TPU v7x, 32 devices: a whole 2x2x4 slice. The times are simulated.
32 devices in a mesh: seg: 8 (over y, x, core), grp: 4 (over z).
Axes of the slice: x: 2, y: 2, z: 4, core: 2. Of those that a mesh axis runs over, the one named last changes fastest.
Arguments:
- strain: bfloat16 [4096, 1792], P(('seg', 'grp')), may hold values from -40 to 40
- counts: int32 [4096], P(('seg', 'grp')), may hold values from 448 to 1792, as said below
- working: int32 [4096], P(('seg', 'grp')), may hold values 0 or 1
- mixing: bfloat16 [512, 512], P('grp'), may hold values from -0.25 to 0.25
- owners: int32 [2], replicated, may hold values from 0 to 31
- offsets: int32 [2], replicated, may hold values from 0 to 64
Outputs:
- correlations: bfloat16 [2, 201, 64, 4096], P(None, None, None, ('seg', 'grp'))
Inputs may be any that keep to these rules, and one draw needn't show every extreme that they name: `counts`: some channel has 1792 valid samples in every draw.
All inputs are finite; a program needn't handle non-finite values. No bound on the sum of `working` on one device may be relied on, other than what follows from the above.
Results may differ from a plain program's by a relative error of at most 0.0058.
Values may be sent and summed in bfloat16 or wider, within the bound.
A program may use at most 64 MiB of HBM per device.

v0:
```python
import jax
import jax.numpy as jnp
from jax import lax
from jax.sharding import PartitionSpec as P

SRC = 64
LAG = 100
ROUNDS = 2
LAGS = 201


epsilon = 1e-05


def broadcast(value, axis, source):
    kept = jnp.where(lax.axis_index(axis) == source, value, 0).astype(value.dtype)
    return lax.psum(kept, axis)


def deliver(sent_block, owner_index):
    arrived = broadcast(sent_block, ("seg", "grp"), owner_index)
    return arrived


def correlate(whitened, source):
    lag_bunch = 8
    lag_groups = -(-LAGS // lag_bunch)
    total_lags = lag_groups * lag_bunch
    samples = whitened.shape[1]
    norm_scale = 1.0 / float(samples) ** 0.5
    source_pad = jnp.pad(source, ((0, 0), (LAG, LAG + total_lags - LAGS)))

    def group_step(unused_state, group_index):
        first_lag = group_index * lag_bunch
        shifted = jnp.stack(
            [
                lax.dynamic_slice_in_dim(source_pad, first_lag + lag_step, samples, 1)
                for lag_step in range(lag_bunch)
            ]
        )
        products = jnp.einsum("ksn,cn->ksc", shifted, whitened, preferred_element_type=jnp.float32)
        return (unused_state, (products * norm_scale).astype(jnp.bfloat16))

    unused_state, stacked = lax.scan(
        group_step, jnp.zeros((), jnp.float32), jnp.arange(lag_groups, dtype=jnp.int32)
    )
    return stacked.reshape(total_lags, source.shape[0], whitened.shape[0])[:LAGS]


def on_device(strain, counts, working, mixing, owners, offsets):
    positions = lax.broadcasted_iota(jnp.int32, strain.shape, 1)
    usable = (positions < counts[:, None]) & (working[:, None] > 0)
    masked = jnp.where(usable, strain, jnp.zeros_like(strain))
    coupled = jnp.dot(
        mixing,
        lax.all_gather(masked, "grp", axis=0, tiled=True),
        preferred_element_type=jnp.float32,
    )
    filtered = jnp.where(usable, masked.astype(jnp.float32) - coupled, jnp.float32(0.0))
    sumsq = jnp.sum(filtered * filtered, axis=1)
    spread = jnp.sqrt(sumsq / counts.astype(jnp.float32) + epsilon)
    whitened = (filtered / spread[:, None]).astype(jnp.bfloat16)
    rounds_out = []
    for round_index in range(ROUNDS):
        owner_index = owners[round_index]
        row_offset = offsets[round_index]
        source = lax.dynamic_slice_in_dim(deliver(whitened, owner_index), row_offset, SRC, 0)
        rounds_out.append(correlate(whitened, source))
    return jnp.stack(rounds_out)


def solution(mesh):
    in_specs = (
        P(("seg", "grp"), None),
        P(("seg", "grp")),
        P(("seg", "grp")),
        P("grp", None),
        P(),
        P(),
    )
    out_specs = P(None, None, None, ("seg", "grp"))
    return jax.shard_map(
        on_device, mesh=mesh, in_specs=in_specs, out_specs=out_specs, check_vma=False
    )
```

profile of v0, /device:TPU:0, one launch (start us, length us, event | category | flops | bytes accessed | tf_op | source)
XLA Modules:
  0.0 404.8 jit_solution(6292009471522378777)
XLA Ops:
  8.5 1.7 fusion.11
  12.0 43.0 %all-gather.2.cloned.1.call-done = bf16[512,1792]{0,1:T(8,128)(2,1)} async-done(((bf16[128,1792]{0,1:T(8,128)(2,1)}), bf16[512,1792]{0,1:T(8,128)(2,1)}) %all-gather.2.cloned.1.call-update) | async-done | bytes 1835024 | tf_op jit(solution)/shard_map/all_gather | solution.py:56
  55.0 2.2 multiply_reduce_fusion
  63.6 124.8 %all-reduce.5.cloned.1.call-done = (bf16[128,1792]{0,1:T(8,128)(2,1)}, bf16[128,1792]{0,1:T(8,128)(2,1)}) async-done(((bf16[128,1792]{0,1:T(8,128)(2,1)}, bf16[128,1792]{0,1:T(8,128)(2,1)}), (bf16[128,1792]{0,1:T(8,128)(2,1)}, bf16[128,1792]{0,1:T(8,128)(2,1)})) %all-reduce.5.cloned.1.call-update) | async-done | bytes 917520 | tf_op jit(solution)/shard_map/psum | solution.py:17
  188.4 1.5 constant_dynamic-slice_fusion
  190.4 2.6 broadcast.23.clone
  193.1 97.4 %while.25 = (s32[]{:T(128)}, bf16[26,8,64,128]{3,2,1,0:T(8,128)(2,1)}, s32[26]{0:T(128)S(1)}, bf16[64,1999]{1,0:T(8,128)(2,1)S(1)}, bf16[128,1792]{1,0:T(8,128)(...) while((s32[]{:T(128)}, ...), condition=%wide.region_6.7_spmd, body=%wide.region_5.6_spmd.sunk | while | flops 235012128 | bytes 6095469 | solution.py:44
  195.5 1.3 fusion.29
  199.2 1.3 fusion.29
  203.0 1.3 fusion.29
  206.7 1.3 fusion.29
  210.5 1.3 fusion.29
  214.2 1.3 fusion.29
  218.0 1.3 fusion.29
  221.7 1.3 fusion.29
  225.5 1.3 fusion.29
  229.2 1.3 fusion.29
  233.0 1.3 fusion.29
  236.7 1.3 fusion.29
  240.4 1.3 fusion.29
  244.2 1.3 fusion.29
  247.9 1.3 fusion.29
  251.7 1.3 fusion.29
  255.4 1.3 fusion.29
  259.2 1.3 fusion.29
  262.9 1.3 fusion.29
  266.7 1.3 fusion.29
  270.4 1.3 fusion.29
  274.1 1.3 fusion.29
  277.9 1.3 fusion.29
  281.6 1.3 fusion.29
  285.4 1.3 fusion.29
  289.1 1.3 fusion.29
  290.4 4.3 %slice_bitcast_fusion = bf16[1,201,64,128]{3,2,1,0:T(8,128)(2,1)} fusion(bf16[208,64,128]{2,1,0:T(8,128)(2,1)} %bitcast.117), kind=kLoop, calls=%fused_computation.27 | loop fusion | bytes 6586368 | tf_op jit(solution)/shard_map/stack | solution.py:69
  294.9 2.6 broadcast.23.clone.1
  297.5 94.1 %while.24 = (s32[]{:T(128)}, bf16[26,8,64,128]{3,2,1,0:T(8,128)(2,1)}, s32[26]{0:T(128)S(1)}, bf16[64,1999]{1,0:T(8,128)(2,1)S(1)}, bf16[128,1792]{1,0:T(8,128)(...) while((s32[]{:T(128)}, ...), condition=%wide.region_3.4_spmd, body=%wide.region_2.3_spmd.sunk | while | flops 235012128 | bytes 6095469 | solution.py:44
  299.8 1.3 fusion.26
  303.5 1.3 fusion.26
  307.1 1.3 fusion.26
  310.7 1.3 fusion.26
  314.3 1.3 fusion.26
  317.9 1.3 fusion.26
  321.6 1.3 fusion.26
  325.2 1.3 fusion.26
  328.8 1.3 fusion.26
  332.4 1.3 fusion.26
  336.1 1.3 fusion.26
  339.7 1.3 fusion.26
  343.3 1.3 fusion.26
  346.9 1.3 fusion.26
  350.5 1.3 fusion.26
  354.2 1.3 fusion.26
  357.8 1.3 fusion.26
  361.4 1.3 fusion.26
  365.0 1.3 fusion.26
  368.6 1.3 fusion.26
  372.3 1.3 fusion.26
  375.9 1.3 fusion.26
  379.5 1.3 fusion.26
  383.1 1.3 fusion.26
  386.7 1.3 fusion.26
  390.4 1.3 fusion.26
  391.7 2.8 slice_bitcast_fusion.1
  394.6 3.4 pad_maximum_fusion
  (496 shorter events, 93.5 us)
Async XLA Ops:
  6.5 48.5 %copy-start = (bf16[128,512]{1,0:T(8,128)(2,1)S(1)}, bf16[128,512]{1,0:T(8,128)(2,1)}, u32[]{:S(2)}) copy-start(bf16[128,512]{1,0:T(8,128)(2,1)} %param.13) | copy-start | bytes 393220
  6.5 48.5 %copy-start.4 = (s32[128]{0:T(128)S(1)}, s32[128]{0:T(128)}, u32[]{:S(2)}) copy-start(s32[128]{0:T(128)} %param.11) | copy-start | bytes 1540
  6.5 3.7 copy-start.2
  6.5 48.5 %all-gather.2.cloned.1.call-start = ((), (), s32[]{:S(2)}) async-start(), calls=%async_computation | async-start | bytes 2293760 | tf_op jit(solution)/shard_map/all_gather | solution.py:56
  10.2 178.2 %all-reduce.5.cloned.1.call-start = ((), (), s32[]{:S(2)}) async-start(), calls=%async_computation.1 | async-start | bytes 1835008 | tf_op jit(solution)/shard_map/psum | solution.py:17
  57.2 1.8 copy-start.3
  391.7 2.9 copy-start.1
Sparse Core Ops, SparseCore 0:
  10.3 44.6 all-gather.1
  60.4 127.9 all-reduce.4
where the time goes:
time: 407 us; the launch traced here: 405 us
  waiting for transfers between devices  168 us (41%)
  local copies, waits for them, and re-layouts  105 us (26%)
  matrix products  69.8 us (17%)
  loops' own time  36.5 us (9%)
  between operations  18.4 us (5%)
  other arithmetic  7.47 us (2%)
    psum x1, waiting for transfers between devices, broadcast(): return lax.psum(kept, axis)  125 us
    dot_general x52, matrix products, group_step(): jnp.einsum('ksn,cn->ksc', shifted, whitened, preferred_element_type=jnp.f...  67.6 us
    while x364, local copies, waits for them, and re-layouts  49.9 us
    all_gather x1, waiting for transfers between devices, on_device(): lax.all_gather(masked, 'grp', axis=0, tiled=True)  43 us
    another operation x2, loops' own time, correlate(): lax.scan(group_step, jnp.zeros((), jnp.float32), jnp.arange(lag_groups, d...  36.5 us
    dynamic_slice x52, local copies, waits for them, and re-layouts, correlate(): lax.scan(group_step, jnp.zeros((), jnp.float32), jnp.arange(lag_groups, d...  30.4 us
  transfers between devices with their start and end apart: 2, of which 2 were waited for; matrix products, arithmetic and copies ran while one was open for 0% of the time, Pallas kernels for 0%

commit v1 on v0

v1 whole, which is shorter than its diff:
```python
import jax
import jax.numpy as jnp
from jax import lax
from jax.experimental import pallas as pl
from jax.experimental.pallas import tpu as pltpu
from jax.sharding import PartitionSpec as P

SRC = 64
LAG = 100
ROUNDS = 2
LAGS = 201
STEP = 10
GROUPS = LAG // STEP
PAD = 128

epsilon = 1e-05
NT = (((1,), (1,)), ((), ()))


def correlate_kernel(w_ref, s_ref, out_ref, wpad, spad, left, right):
    channels, samples = w_ref.shape
    rows = s_ref.shape[0]
    scale = 1.0 / float(samples) ** 0.5
    for pad, ref in ((wpad, w_ref), (spad, s_ref)):
        edge = jnp.zeros((ref.shape[0], PAD), ref.dtype)
        pad[:, :PAD] = edge
        pad[:, PAD + samples :] = edge
        pad[:, PAD : PAD + samples] = ref[...]
    for sign_index, sign in enumerate((1, -1)):
        for group in range(GROUPS):
            start = PAD + sign * STEP * group
            left[sign_index, group * rows : (group + 1) * rows, :] = spad[:, start : start + samples]
        for delta in range(STEP):
            start = PAD - sign * (delta + 1)
            right[sign_index * STEP + delta] = wpad[:, start : start + samples]

    centre = lax.dot_general(s_ref[...], w_ref[...], NT, preferred_element_type=jnp.float32)
    centre = (centre * scale).astype(jnp.bfloat16)
    for r in range(ROUNDS):
        out_ref[r, LAG] = centre[r * SRC : (r + 1) * SRC]

    def tile(n, carry):
        sign_index = n // (STEP // 2)
        sign = 1 - 2 * sign_index
        first = (n % (STEP // 2)) * 2
        pair = right[pl.ds(n * 2, 2)].reshape(2 * channels, samples)
        products = lax.dot_general(left[sign_index], pair, NT, preferred_element_type=jnp.float32)
        products = (products * scale).astype(jnp.bfloat16)
        for group in range(GROUPS):
            for r in range(ROUNDS):
                row = group * rows + r * SRC
                for d in range(2):
                    lag = LAG + sign * (STEP * group + first + d + 1)
                    out_ref[r, lag] = products[row : row + SRC, d * channels : (d + 1) * channels]
        return carry

    lax.fori_loop(0, STEP, tile, 0)


def correlate(whitened, sources):
    channels, samples = whitened.shape
    rows = sources.shape[0]
    return pl.pallas_call(
        correlate_kernel,
        out_shape=jax.ShapeDtypeStruct((ROUNDS, LAGS, SRC, channels), jnp.bfloat16),
        in_specs=[pl.BlockSpec(memory_space=pltpu.VMEM)] * 2,
        out_specs=pl.BlockSpec(memory_space=pltpu.VMEM),
        scratch_shapes=[
            pltpu.VMEM((channels, samples + 2 * PAD), jnp.bfloat16),
            pltpu.VMEM((rows, samples + 2 * PAD), jnp.bfloat16),
            pltpu.VMEM((2, GROUPS * rows, samples), jnp.bfloat16),
            pltpu.VMEM((2 * STEP, channels, samples), jnp.bfloat16),
        ],
        compiler_params=pltpu.CompilerParams(vmem_limit_bytes=52 * 1024 * 1024),
        cost_estimate=pl.CostEstimate(
            flops=2 * LAGS * rows * channels * samples, bytes_accessed=8 << 20, transcendentals=0
        ),
        name="correlate",
    )(whitened, sources)


def on_device(strain, counts, working, mixing, owners, offsets):
    positions = lax.broadcasted_iota(jnp.int32, strain.shape, 1)
    usable = (positions < counts[:, None]) & (working[:, None] > 0)
    masked = jnp.where(usable, strain, jnp.zeros_like(strain))
    coupled = jnp.dot(
        mixing,
        lax.all_gather(masked, "grp", axis=0, tiled=True),
        preferred_element_type=jnp.float32,
    )
    filtered = jnp.where(usable, masked.astype(jnp.float32) - coupled, jnp.float32(0.0))
    sumsq = jnp.sum(filtered * filtered, axis=1)
    spread = jnp.sqrt(sumsq / counts.astype(jnp.float32) + epsilon)
    whitened = (filtered / spread[:, None]).astype(jnp.bfloat16)
    me = lax.axis_index(("seg", "grp"))
    mine = [
        jnp.where(me == owners[r], lax.dynamic_slice_in_dim(whitened, offsets[r], SRC, 0), 0)
        for r in range(ROUNDS)
    ]
    sources = lax.psum(jnp.concatenate(mine, axis=0).astype(jnp.bfloat16), ("seg", "grp"))
    return correlate(whitened, sources)


def solution(mesh):
    in_specs = (
        P(("seg", "grp"), None),
        P(("seg", "grp")),
        P(("seg", "grp")),
        P("grp", None),
        P(),
        P(),
    )
    out_specs = P(None, None, None, ("seg", "grp"))
    return jax.shard_map(
        on_device, mesh=mesh, in_specs=in_specs, out_specs=out_specs, check_vma=False
    )
```

time: 407 us -> 215 us (0.53)
  local copies, waits for them, and re-layouts: 105 us -> 3.79 us
  matrix products: 69.8 us -> 2.32 us
  loops' own time: 36.5 us -> 0 us
  Pallas kernels: 0 us -> 22 us
  waiting for transfers between devices: 168 us -> 163 us
    dot_general x52 -> x0, matrix products: 67.6 us -> none  [group_step(): jnp.einsum('ksn,cn->ksc', shifted, whitened, preferred_element_type=jnp.f...]
    while x365 -> x0, local copies, waits for them, and re-layouts: 50.1 us -> none
    another operation x2 -> x0, loops' own time: 36.5 us -> none  [correlate(): lax.scan(group_step, jnp.zeros((), jnp.float32), jnp.arange(lag_groups, d...]
    dynamic_slice x53 -> x0, local copies, waits for them, and re-layouts: 31.9 us -> none  [the longest x52 30.4 us: correlate(): lax.scan(group_step, jnp.zeros((), jnp.float32), jnp.arange(lag_groups, d...]
    pallas_call x0 -> x1, Pallas kernels: none -> 22 us  [correlate(): pl.pallas_call(correlate_kernel, out_shape=jax.ShapeDtypeStruct((ROUNDS,...]
    another operation x56 -> x0, local copies, waits for them, and re-layouts: 19.5 us -> none  [the longest x2 7.15 us: on_device(): return jnp.stack(rounds_out)]
    all_gather x1, waiting for transfers between devices: 43 us -> 36.4 us  [on_device(): lax.all_gather(masked, 'grp', axis=0, tiled=True)]
  transfers between devices with their start and end apart: 2 -> 2, of which waited for: 2 -> 2; matrix products, arithmetic and copies ran while one was open for 0% -> 1% of each run, Pallas kernels for 0% -> 0%
where the time goes in v1:
time: 215 us; the launch traced here: 214 us
  waiting for transfers between devices  163 us (76%)
  Pallas kernels  22 us (10%)
  between operations  18.5 us (9%)
  other arithmetic  3.95 us (2%)
  local copies, waits for them, and re-layouts  3.79 us (2%)
  matrix products  2.32 us (1%)
    psum x1, waiting for transfers between devices, on_device(): lax.psum(jnp.concatenate(mine, axis=0).astype(jnp.bfloat16), ('seg', 'grp'))  127 us
    all_gather x1, waiting for transfers between devices, on_device(): lax.all_gather(masked, 'grp', axis=0, tiled=True)  36.4 us
    pallas_call x1, Pallas kernels, correlate(): pl.pallas_call(correlate_kernel, out_shape=jax.ShapeDtypeStruct((ROUNDS,...  22 us
  transfers between devices with their start and end apart: 2, of which 2 were waited for; matrix products, arithmetic and copies ran while one was open for 1% of the time, Pallas kernels for 0%

profile of v1, /device:TPU:0, one launch (start us, length us, event | category | flops | bytes accessed | tf_op | source)
XLA Modules:
  0.0 213.7 jit_solution(6666604308045375378)
XLA Ops:
  6.5 0.0 copy-start
  6.5 0.0 all-gather.2.cloned.1.call-start
  6.5 0.7 broadcast_compare_fusion
  7.2 2.2 %fusion.3 = bf16[128,1792]{1,0:T(8,128)(2,1)} fusion(bf16[128,1792]{1,0:T(8,128)(2,1)} %param.6, s32[128]{0:T(128)} %param.7, pred[128]{0:T(512)(128)(4,1)S(1)} %broadcast_compare_fusion), kind=kLoop, calls=%fused_computation.7 | loop fusion | flops 688128 | bytes 918144 | tf_op jit(solution)/shard_map/jit(_where)/select_n | solution.py:85
  9.4 0.0 all-gather.2.cloned.1.call-update
  9.4 0.0 all-reduce.2.cloned.1.call-start
  9.5 1.4 fusion.5
  13.4 1.4 fusion.4
  17.3 0.0 copy-start.2
  17.3 36.4 %all-gather.2.cloned.1.call-done = bf16[512,1792]{1,0:T(8,128)(2,1)} async-done(((bf16[128,1792]{1,0:T(8,128)(2,1)}), bf16[512,1792]{1,0:T(8,128)(2,1)}) %all-gather.2.cloned.1.call-update) | async-done | bytes 1835024 | tf_op jit(solution)/shard_map/all_gather | solution.py:88
  53.7 0.0 copy-done
  53.7 2.3 %multiply_reduce_fusion = (f32[128]{0:T(128)S(1)}, f32[128,1792]{1,0:T(8,128)S(1)}) fusion(bf16[128,512]{1,0:T(8,128)(2,1)S(1)} %copy-done, bf16[512,1792]{1,0:T(8,128)(2,1)} %all-gather.2.cloned.1.call-done, bf16[128,1792]{1,0:T(8,128)(2,1)} %param.6, pred[128]{0:T(512)(128)(4,1)S(1)} %broadcast_compare_fusion, s32[128]{0:T(128)} %param.7), kind=kOutput, calls=%fused_computation.4 | convolution fusion | flops 236715904 | bytes 3343488 | tf_op jit(solution)/shard_map/dot_general | solution.py:86
  56.0 0.0 copy-done.2
  56.0 0.1 divide_convert_fusion.w_ref
  56.2 0.2 dynamic-slice_select_fusion.1
  56.3 0.8 pad_maximum_fusion
  57.1 0.0 all-reduce.2.cloned.1.call-update
  57.1 126.7 %all-reduce.2.cloned.1.call-done.s_ref = bf16[128,1792]{1,0:T(8,128)(2,1)} async-done(((bf16[128,1792]{1,0:T(8,128)(2,1)}), bf16[128,1792]{1,0:T(8,128)(2,1)}) %all-reduce.2.cloned.1.call-update) | async-done | bytes 458768 | tf_op jit(solution)/shard_map/psum | solution.py:100
  183.9 0.0 copy-start.1
  183.9 1.0 copy-done.1
  184.9 22.0 %correlate.1 = bf16[2,201,64,128]{3,2,1,0:T(8,128)(2,1)} custom-call(bf16[128,1792]{1,0:T(8,128)(2,1)S(1)} %divide_convert_fusion.w_ref, bf16[128,1792]{1,0:T(8,128)(2,1)S(1)} %copy-done.1), custom_call_target="tpu_custom_call" | custom-call | flops 11802771456 | bytes 8388608 | tf_op jit(solution)/shard_map/correlate/pallas_call | solution.py:63
  (1 shorter events, 0.0 us)
Async XLA Ops:
  6.5 47.1 %copy-start = (bf16[128,512]{1,0:T(8,128)(2,1)S(1)}, bf16[128,512]{1,0:T(8,128)(2,1)}, u32[]{:S(2)}) copy-start(bf16[128,512]{1,0:T(8,128)(2,1)} %param.9) | copy-start | bytes 393220
  6.5 47.1 %all-gather.2.cloned.1.call-start = ((), (), s32[]{:S(2)}) async-start(), calls=%async_computation | async-start | bytes 2293760 | tf_op jit(solution)/shard_map/all_gather | solution.py:88
  9.4 174.4 %all-reduce.2.cloned.1.call-start = ((), (), s32[]{:S(2)}) async-start(), calls=%async_computation.1 | async-start | bytes 917504 | tf_op jit(solution)/shard_map/psum | solution.py:100
  17.3 38.7 %copy-start.2 = (s32[128]{0:T(128)S(1)}, s32[128]{0:T(128)}, u32[]{:S(2)}) copy-start(s32[128]{0:T(128)} %param.7) | copy-start | bytes 1540
  183.9 1.0 copy-start.1
Sparse Core Ops, SparseCore 0:
  9.5 44.0 all-gather.1
  59.0 124.8 all-reduce.1

commit v2 on v1

--- a/solution.py
+++ b/solution.py
@@ -79,7 +79,231 @@
     )(whitened, sources)
 
 
-def on_device(strain, counts, working, mixing, owners, offsets):
+CHUNKS = 7
+META = 16
+XI, XE, EX, FE, SA, SB, SC, SE = range(8)
+MESH = pl.DeviceIdType.MESH
+
+
+def counts_column(meta, n):
+    lanes = meta[0:1, :n].astype(jnp.float32) * 8.0 + meta[1:2, :n].astype(jnp.float32)
+    row = lax.broadcasted_iota(jnp.int32, (n, n), 0)
+    lane = lax.broadcasted_iota(jnp.int32, (n, n), 1)
+    return jnp.sum(jnp.where(row == lane, lanes, 0.0), axis=1, keepdims=True)
+
+
+def gather_kernel(strain, mext, msel, pick, w_out, s_out, xall, fown, fe, sa, ra, sb, rb, sc, rc,
+                  s_all, mext_end, msel_end, msel_sum, msel_far, left, send, recv, msend, mrecv):
+    n, samples = strain.shape
+    width = samples // CHUNKS
+    seg = lax.axis_index("seg")
+    z = lax.axis_index("grp")
+    is_end = (z % 3) == 0
+    near = 1 + z // 3
+    end = 3 * (z - 1)
+    far = 3 - z
+    far_end = 3 - end
+    flips = [seg + 1 - 2 * (seg % 2), seg + 2 - 4 * ((seg // 2) % 2), seg + 4 - 8 * (seg // 4)]
+
+    def cols(c):
+        return pl.ds(c * width, width)
+
+    def copy(src, dst, kind, c, device):
+        return pltpu.make_async_remote_copy(
+            src_ref=src, dst_ref=dst, send_sem=send.at[kind, c], recv_sem=recv.at[kind, c],
+            device_id=device, device_id_type=MESH)
+
+    def block(index, c):
+        return xall.at[pl.ds(index * n, n), cols(c)]
+
+    def x_copy(index, kind, c, target):
+        return copy(block(index, c), block(index, c), kind, c, {"grp": target})
+
+    def part_copy(src, dst, kind, c, device):
+        return copy(src.at[:, cols(c)], dst.at[:, cols(c)], kind, c, device)
+
+    def m_copy(src, dst, index, target):
+        return pltpu.make_async_remote_copy(
+            src_ref=src, dst_ref=dst, send_sem=msend.at[index], recv_sem=mrecv.at[index],
+            device_id={"grp": target}, device_id_type=MESH)
+
+    barrier = pltpu.get_barrier_semaphore()
+    own_counts = counts_column(mext[n:], n)
+
+    def usable(counts, c):
+        position = lax.broadcasted_iota(jnp.int32, (n, width), 1) + c * width
+        return position.astype(jnp.float32) < counts
+
+    def mask_own(c):
+        part = jnp.where(usable(own_counts, c), strain[:, c * width : (c + 1) * width].astype(jnp.float32), 0.0)
+        xall[pl.ds(z * n, n), c * width : (c + 1) * width] = part.astype(jnp.bfloat16)
+
+    def whiten(out, ref, counts):
+        total = jnp.zeros((n, 1), jnp.float32)
+        for c in range(CHUNKS):
+            part = ref[:n, c * width : (c + 1) * width].astype(jnp.float32)
+            total += jnp.sum(part * part, axis=1, keepdims=True)
+        gain = 1.0 / jnp.sqrt(total / jnp.maximum(counts, 1.0) + epsilon)
+        for c in range(CHUNKS):
+            part = ref[:n, c * width : (c + 1) * width].astype(jnp.float32)
+            out[:, c * width : (c + 1) * width] = (part * gain).astype(jnp.bfloat16)
+
+    @pl.when(is_end)
+    def _():
+        pl.semaphore_signal(barrier, inc=1, device_id={"grp": near}, device_id_type=MESH)
+        pl.semaphore_wait(barrier, 1)
+        sends = []
+
+        def go(c):
+            sends.append(c)
+            c.start()
+
+        mask_own(0)
+        go(x_copy(z, EX, 0, near))
+        go(m_copy(msel, msel_end, 0, near))
+        mask_own(1)
+        go(x_copy(z, EX, 1, near))
+        go(m_copy(mext, mext_end, 1, near))
+        for c in range(2, CHUNKS):
+            mask_own(c)
+            go(x_copy(z, EX, c, near))
+        for c in range(CHUNKS):
+            part_copy(fe, fe, FE, c, {"grp": near}).wait_recv()
+            part_copy(s_all, s_all, SE, c, {"grp": near}).wait_recv()
+        for c in sends:
+            c.wait_send()
+        whiten(w_out, fe, own_counts)
+
+    @pl.when(jnp.logical_not(is_end))
+    def _():
+        for target in (end, far):
+            pl.semaphore_signal(barrier, inc=1, device_id={"grp": target}, device_id_type=MESH)
+        for target in flips:
+            pl.semaphore_signal(barrier, inc=1, device_id={"seg": target}, device_id_type=MESH)
+        pl.semaphore_wait(barrier, 5)
+        sends = []
+
+        def go(c):
+            sends.append(c)
+            c.start()
+
+        def forward(c):
+            x_copy(end, EX, c, end).wait_recv()
+            go(x_copy(end, XE, c, far))
+
+        def send_own(c):
+            mask_own(c)
+            go(x_copy(z, XI, c, far))
+
+        send_own(0)
+        send_own(1)
+        forward(0)
+        m_copy(msel_end, msel_end, 0, end).wait_recv()
+        msel_sum[...] = msel[...] + msel_end[...]
+        go(m_copy(msel_sum, msel_far, 2, far))
+        forward(1)
+        send_own(2)
+        m_copy(mext_end, mext_end, 1, end).wait_recv()
+        left[:n] = mext[:n]
+        left[n : 2 * n] = mext_end[:n]
+        end_counts = counts_column(mext_end[n:], n)
+        m_copy(msel_far, msel_far, 2, far).wait_recv()
+        left[2 * n : 3 * n] = msel_sum[:n] + msel_far[:n]
+        left[3 * n :] = pick[...]
+        meta = msel_sum[n:] + msel_far[n:]
+        src_counts = counts_column(meta, n)
+        sa[n:] = jnp.zeros((META, samples), jnp.bfloat16)
+        sa[n:, :n] = meta[:, :n]
+
+        def process(c):
+            a, b = c * width, (c + 1) * width
+            x_copy(far, XI, c, far).wait_recv()
+            x_copy(far_end, XE, c, far).wait_recv()
+            coupled = jnp.dot(left[...], xall[:, a:b], preferred_element_type=jnp.float32)
+            own_x = xall[pl.ds(z * n, n), a:b].astype(jnp.float32)
+            end_x = xall[pl.ds(end * n, n), a:b].astype(jnp.float32)
+            fe[:, a:b] = jnp.where(usable(end_counts, c), end_x - coupled[n : 2 * n], 0.0).astype(jnp.bfloat16)
+            part = jnp.where(usable(src_counts, c), coupled[3 * n :] - coupled[2 * n : 3 * n], 0.0)
+            sa[:n, a:b] = part.astype(jnp.bfloat16)
+            go(part_copy(sa, ra, SA, c, {"seg": flips[0]}))
+            go(part_copy(fe, fe, FE, c, {"grp": end}))
+            fown[:, a:b] = jnp.where(usable(own_counts, c), own_x - coupled[:n], 0.0)
+
+        def stage(mine, arrived, total, kind, c, flip):
+            a, b = c * width, (c + 1) * width
+            part_copy(mine, arrived, kind, c, {"seg": flip}).wait_recv()
+            total[:, a:b] = mine[:, a:b] + arrived[:, a:b]
+
+        for step in range(CHUNKS + 3):
+            if step + 2 < CHUNKS:
+                forward(step + 2)
+            if step + 3 < CHUNKS:
+                send_own(step + 3)
+            if step < CHUNKS:
+                process(step)
+            if 0 <= step - 1 < CHUNKS:
+                stage(sa, ra, sb, SA, step - 1, flips[0])
+                go(part_copy(sb, rb, SB, step - 1, {"seg": flips[1]}))
+            if 0 <= step - 2 < CHUNKS:
+                stage(sb, rb, sc, SB, step - 2, flips[1])
+                go(part_copy(sc, rc, SC, step - 2, {"seg": flips[2]}))
+            if 0 <= step - 3 < CHUNKS:
+                stage(sc, rc, s_all, SC, step - 3, flips[2])
+                go(part_copy(s_all, s_all, SE, step - 3, {"grp": end}))
+        whiten(w_out, fown, own_counts)
+        for c in sends:
+            c.wait_send()
+
+    whiten(s_out, s_all, counts_column(s_all[n:, :n], n))
+
+
+def gather(strain, counts, working, mixing, owners, offsets):
+    n, samples = strain.shape
+    wide = mixing.shape[1]
+    me = lax.axis_index(("seg", "grp"))
+    groups = wide // n
+    group = lax.axis_index("seg")
+    eff = jnp.where(working > 0, counts, 0)
+    meta = jnp.stack([eff // 8, eff % 8]).astype(jnp.bfloat16)
+    mext = jnp.concatenate([mixing, jnp.pad(meta, ((0, META - 2), (0, wide - n)))], axis=0)
+    rows, metas, picks = [], [], []
+    for r in range(ROUNDS):
+        here = me == owners[r]
+        rows.append(jnp.where(here, lax.dynamic_slice_in_dim(mixing, offsets[r], SRC, 0), 0))
+        metas.append(jnp.where(here, lax.dynamic_slice_in_dim(meta, offsets[r], SRC, 1), 0))
+        first = jnp.where(owners[r] // groups == group, (owners[r] % groups) * n + offsets[r], -wide)
+        column = lax.broadcasted_iota(jnp.int32, (SRC, wide), 1)
+        row = lax.broadcasted_iota(jnp.int32, (SRC, wide), 0)
+        picks.append(column == row + first)
+    sel_meta = jnp.concatenate(metas, axis=1)
+    msel = jnp.concatenate(rows + [jnp.pad(sel_meta, ((0, META - 2), (0, wide - n)))], axis=0).astype(jnp.bfloat16)
+    pick = jnp.concatenate(picks, axis=0).astype(jnp.bfloat16)
+    vmem = pl.BlockSpec(memory_space=pltpu.VMEM)
+    part = pltpu.VMEM((n + META, samples), jnp.bfloat16)
+    mat = pltpu.VMEM((n + META, wide), jnp.bfloat16)
+    return pl.pallas_call(
+        gather_kernel,
+        out_shape=[jax.ShapeDtypeStruct((n, samples), jnp.bfloat16)] * 2,
+        in_specs=[vmem] * 4,
+        out_specs=[vmem] * 2,
+        scratch_shapes=[
+            pltpu.VMEM((wide, samples), jnp.bfloat16),
+            pltpu.VMEM((n, samples), jnp.float32),
+            pltpu.VMEM((n, samples), jnp.bfloat16),
+        ] + [part] * 7 + [mat] * 4 + [
+            pltpu.VMEM((4 * n, wide), jnp.bfloat16),
+            pltpu.SemaphoreType.DMA((8, CHUNKS)),
+            pltpu.SemaphoreType.DMA((8, CHUNKS)),
+            pltpu.SemaphoreType.DMA((3,)),
+            pltpu.SemaphoreType.DMA((3,)),
+        ],
+        compiler_params=pltpu.CompilerParams(
+            collective_id=0, has_side_effects=True, vmem_limit_bytes=32 * 1024 * 1024),
+        name="gather",
+    )(strain, mext, msel, pick)
+
+
+def gather_any(strain, counts, working, mixing, owners, offsets):
     positions = lax.broadcasted_iota(jnp.int32, strain.shape, 1)
     usable = (positions < counts[:, None]) & (working[:, None] > 0)
     masked = jnp.where(usable, strain, jnp.zeros_like(strain))
@@ -98,6 +322,12 @@
         for r in range(ROUNDS)
     ]
     sources = lax.psum(jnp.concatenate(mine, axis=0).astype(jnp.bfloat16), ("seg", "grp"))
+    return whitened, sources
+
+
+def on_device(strain, counts, working, mixing, owners, offsets):
+    fits = lax.axis_size("seg") == 8 and lax.axis_size("grp") == 4
+    whitened, sources = (gather if fits else gather_any)(strain, counts, working, mixing, owners, offsets)
     return correlate(whitened, sources)
 
 

time: 215 us -> 87.8 us (0.41)
  waiting for transfers between devices: 163 us -> 0 us
  Pallas kernels: 22 us -> 68.6 us
  between operations: 18.5 us -> 12.1 us
  matrix products: 2.32 us -> 0 us
    psum x1 -> x0, waiting for transfers between devices: 127 us -> none  [on_device(): lax.psum(jnp.concatenate(mine, axis=0).astype(jnp.bfloat16), ('seg', 'grp'))]
    pallas_call x0 -> x1, Pallas kernels: none -> 46.8 us  [gather(): pl.pallas_call(gather_kernel, out_shape=[jax.ShapeDtypeStruct((n, samples...]
    all_gather x1 -> x0, waiting for transfers between devices: 36.4 us -> none  [on_device(): lax.all_gather(masked, 'grp', axis=0, tiled=True)]
    dot_general x1 -> x0, matrix products: 2.32 us -> none  [on_device(): jnp.dot(mixing, lax.all_gather(masked, 'grp', axis=0, tiled=True), prefer...]
  transfers between devices with their start and end apart: 2 -> 0, of which waited for: 2 -> 0; matrix products, arithmetic and copies ran while one was open for 1% -> 0% of each run, Pallas kernels for 0% -> 0%
where the time goes in v2:
time: 87.8 us; the launch traced here: 87.4 us
  Pallas kernels  68.6 us (78%)
  between operations  12.1 us (14%)
  local copies, waits for them, and re-layouts  3.78 us (4%)
  other arithmetic  2.93 us (3%)
    pallas_call x1, Pallas kernels, gather(): pl.pallas_call(gather_kernel, out_shape=[jax.ShapeDtypeStruct((n, samples...  46.8 us
    pallas_call x1, Pallas kernels, correlate(): pl.pallas_call(correlate_kernel, out_shape=jax.ShapeDtypeStruct((ROUNDS,...  21.8 us

profile of v2, /device:TPU:0, one launch (start us, length us, event | category | flops | bytes accessed | tf_op | source)
XLA Modules:
  0.0 87.4 jit_solution(5350038123826937904)
XLA Ops:
  0.0 0.7 convert_bitcast_fusion
  0.7 1.4 %fusion.11 = (s32[1]{0:T(128)}, s32[1]{0:T(128)}) fusion(s32[2]{0:T(128)} %param.10), kind=kLoop, calls=%fused_computation.34 | loop fusion | bytes 16 | tf_op jit(solution)/shard_map/slice | solution.py:271
  8.8 1.4 %fusion.10 = (s32[1]{0:T(128)}, s32[1]{0:T(128)}) fusion(s32[2]{0:T(128)} %param.11), kind=kLoop, calls=%fused_computation.33 | loop fusion | bytes 16 | tf_op jit(solution)/shard_map/slice | solution.py:272
  15.5 0.1 broadcast_select_fusion.1
  15.6 0.1 fusion.7
  15.7 0.1 iota_compare_fusion.1
  15.8 1.0 %dynamic-slice_select_fusion.1 = (bf16[64,512]{1,0:T(8,128)(2,1)S(1)}, bf16[64,512]{1,0:T(8,128)(2,1)S(1)}) fusion(bf16[128,512]{1,0:T(8,128)(2,1)} %param.9, s32[]{:T(128)S(6)} %select_n.80, pred[]{:T(512)S(6)} %eq.23, s32[]{:T(128)S(6)} %select_n.83, pred[]{:T(512)S(6)} %eq.24), kind=kLoop, calls=%fused_computation.8 | loop fusion | flops 65536 | bytes 262154 | tf_op jit(solution)/shard_map/jit(_where)/select_n | solution.py:272
  16.8 0.9 %fusion.1 = (bf16[144,512]{1,0:T(8,128)(2,1)S(1)}, bf16[144,512]{1,0:T(8,128)(2,1)S(1)}) fusion(bf16[2,128]{1,0:T(2,128)(2,1)S(1)} %pad_maximum_fusion.1, bf16[128,512]{1,0:T(8,128)(2,1)} %param.9, bf16[16,512]{1,0:T(8,128)(2,1)S(1)} %fusion.7, bf16[64,512]{1,0:T(8,128)(2,1)S(1)} %get-tuple-element.12, bf16[64,512]{1,0:T(8,128)(2,1)S(1)} %get-tuple-element.11), kind=kLoop, calls=%fused_computation.3 | loop fusion | flops 884736 | bytes 573952 | tf_op jit(solution)/shard_map/concatenate | solution.py:268
  17.8 0.0 copy-start
  17.8 1.0 %copy-done = bf16[128,1792]{1,0:T(8,128)(2,1)S(1)} copy-done((bf16[128,1792]{1,0:T(8,128)(2,1)S(1)}, bf16[128,1792]{1,0:T(8,128)(2,1)}, u32[]{:S(2)}) %copy-start) | copy-done | bytes 458776
  18.8 46.8 %gather.1 = (bf16[128,1792]{1,0:T(8,128)(2,1)S(1)}, bf16[128,1792]{1,0:T(8,128)(2,1)S(1)}) custom-call(bf16[128,1792]{1,0:T(8,128)(2,1)S(1)} %copy-done, bf16[144,512]{1,0:T(8,128)(2,1)S(1)} %get-tuple-element.21.mext, bf16[144,512]{1,0:T(8,128)(2,1)S(1)} %get-tuple-element.22.msel, bf16[128,512]{1,0:T(8,128)(2,1)S(1)} %add_convert_fusion.pick), custom_call_target="tpu_custom_call" | custom-call | tf_op jit(solution)/shard_map/gather/pallas_call | solution.py:284
  65.6 21.8 %correlate.1 = bf16[2,201,64,128]{3,2,1,0:T(8,128)(2,1)} custom-call(bf16[128,1792]{1,0:T(8,128)(2,1)S(1)} %get-tuple-element.7.w_ref, bf16[128,1792]{1,0:T(8,128)(2,1)S(1)} %get-tuple-element.8.s_ref), custom_call_target="tpu_custom_call" | custom-call | flops 11802771456 | bytes 8388608 | tf_op jit(solution)/shard_map/correlate/pallas_call | solution.py:63
  (5 shorter events, 0.0 us)
Async XLA Ops:
  17.8 1.0 %copy-start = (bf16[128,1792]{1,0:T(8,128)(2,1)S(1)}, bf16[128,1792]{1,0:T(8,128)(2,1)}, u32[]{:S(2)}) copy-start(bf16[128,1792]{1,0:T(8,128)(2,1)} %strain.1) | copy-start | bytes 1376260

commit v3 on v2

--- a/solution.py
+++ b/solution.py
@@ -17,7 +17,7 @@
 NT = (((1,), (1,)), ((), ()))
 
 
-def correlate_kernel(w_ref, s_ref, out_ref, wpad, spad, left, right):
+def correlate_kernel(w_ref, s_ref, out_hbm, out_ref, wpad, spad, left, right, sem):
     channels, samples = w_ref.shape
     rows = s_ref.shape[0]
     scale = 1.0 / float(samples) ** 0.5
@@ -38,6 +38,7 @@
     centre = (centre * scale).astype(jnp.bfloat16)
     for r in range(ROUNDS):
         out_ref[r, LAG] = centre[r * SRC : (r + 1) * SRC]
+        pltpu.make_async_copy(out_ref.at[r, LAG], out_hbm.at[r, LAG], sem).start()
 
     def tile(n, carry):
         sign_index = n // (STEP // 2)
@@ -52,9 +53,13 @@
                 for d in range(2):
                     lag = LAG + sign * (STEP * group + first + d + 1)
                     out_ref[r, lag] = products[row : row + SRC, d * channels : (d + 1) * channels]
+                low = LAG + sign * (STEP * group + first) + 1 - 3 * sign_index
+                slab = (r, pl.ds(low, 2))
+                pltpu.make_async_copy(out_ref.at[slab], out_hbm.at[slab], sem).start()
         return carry
 
     lax.fori_loop(0, STEP, tile, 0)
+    pltpu.make_async_copy(out_ref, out_hbm, sem).wait()
 
 
 def correlate(whitened, sources):
@@ -64,12 +69,14 @@
         correlate_kernel,
         out_shape=jax.ShapeDtypeStruct((ROUNDS, LAGS, SRC, channels), jnp.bfloat16),
         in_specs=[pl.BlockSpec(memory_space=pltpu.VMEM)] * 2,
-        out_specs=pl.BlockSpec(memory_space=pltpu.VMEM),
+        out_specs=pl.BlockSpec(memory_space=pl.ANY),
         scratch_shapes=[
+            pltpu.VMEM((ROUNDS, LAGS, SRC, channels), jnp.bfloat16),
             pltpu.VMEM((channels, samples + 2 * PAD), jnp.bfloat16),
             pltpu.VMEM((rows, samples + 2 * PAD), jnp.bfloat16),
             pltpu.VMEM((2, GROUPS * rows, samples), jnp.bfloat16),
             pltpu.VMEM((2 * STEP, channels, samples), jnp.bfloat16),
+            pltpu.SemaphoreType.DMA,
         ],
         compiler_params=pltpu.CompilerParams(vmem_limit_bytes=52 * 1024 * 1024),
         cost_estimate=pl.CostEstimate(
@@ -79,7 +86,8 @@
     )(whitened, sources)
 
 
-CHUNKS = 7
+EDGES = (0, 2, 4, 6, 8, 10, 12, 13, 14)
+CHUNKS = len(EDGES) - 1
 META = 16
 XI, XE, EX, FE, SA, SB, SC, SE = range(8)
 MESH = pl.DeviceIdType.MESH
@@ -92,10 +100,12 @@
     return jnp.sum(jnp.where(row == lane, lanes, 0.0), axis=1, keepdims=True)
 
 
-def gather_kernel(strain, mext, msel, pick, w_out, s_out, xall, fown, fe, sa, ra, sb, rb, sc, rc,
+def gather_kernel(owners, offsets, strain, counts, working, mixing, w_out, s_out, mext, msel, xall, fown, fe, sa, ra, sb, rb, sc, rc,
                   s_all, mext_end, msel_end, msel_sum, msel_far, left, send, recv, msend, mrecv):
     n, samples = strain.shape
-    width = samples // CHUNKS
+    wide = mixing.shape[1]
+    unit = samples // EDGES[-1]
+    edges = [unit * e for e in EDGES]
     seg = lax.axis_index("seg")
     z = lax.axis_index("grp")
     is_end = (z % 3) == 0
@@ -106,7 +116,7 @@
     flips = [seg + 1 - 2 * (seg % 2), seg + 2 - 4 * ((seg // 2) % 2), seg + 4 - 8 * (seg // 4)]
 
     def cols(c):
-        return pl.ds(c * width, width)
+        return pl.ds(edges[c], edges[c + 1] - edges[c])
 
     def copy(src, dst, kind, c, device):
         return pltpu.make_async_remote_copy(
@@ -128,25 +138,46 @@
             device_id={"grp": target}, device_id_type=MESH)
 
     barrier = pltpu.get_barrier_semaphore()
-    own_counts = counts_column(mext[n:], n)
+    live = jnp.where(working[...] > 0, counts[...], 0)
+    high = live // 8
+    row = lax.broadcasted_iota(jnp.int32, (META, n), 0)
+    meta = jnp.where(row == 0, high, jnp.where(row == 1, live - 8 * high, 0)).astype(jnp.float32).astype(jnp.bfloat16)
+    mext[:n] = mixing[...]
+    mext[n:] = jnp.zeros((META, wide), jnp.bfloat16)
+    mext[n:, :n] = meta
+    own_counts = counts_column(meta, n)
+    me = seg * (wide // n) + z
+    chosen, picked = [], []
+    for r in range(ROUNDS):
+        row = lax.broadcasted_iota(jnp.int32, (SRC, wide), 0)
+        column = lax.broadcasted_iota(jnp.int32, (SRC, wide), 1)
+        place = (owners[r] - seg * (wide // n)) * n + offsets[r]
+        picked.append(jnp.where(column == row + place, 1.0, 0.0))
+        place = (owners[r] - me) * (2 * wide) + offsets[r]
+        chosen.append(jnp.where(column[:, :n] == row[:, :n] + place, 1.0, 0.0))
+    pick = jnp.concatenate(picked, axis=0).astype(jnp.bfloat16)
+    chosen = jnp.concatenate(chosen, axis=0).astype(jnp.bfloat16)
+    msel[:n] = jnp.dot(chosen, mixing[...], preferred_element_type=jnp.float32).astype(jnp.bfloat16)
+    msel[n:] = jnp.zeros((META, wide), jnp.bfloat16)
+    msel[n:, :n] = lax.dot_general(meta, chosen, NT, preferred_element_type=jnp.float32).astype(jnp.bfloat16)
 
     def usable(counts, c):
-        position = lax.broadcasted_iota(jnp.int32, (n, width), 1) + c * width
+        position = lax.broadcasted_iota(jnp.int32, (n, edges[c + 1] - edges[c]), 1) + edges[c]
         return position.astype(jnp.float32) < counts
 
     def mask_own(c):
-        part = jnp.where(usable(own_counts, c), strain[:, c * width : (c + 1) * width].astype(jnp.float32), 0.0)
-        xall[pl.ds(z * n, n), c * width : (c + 1) * width] = part.astype(jnp.bfloat16)
-
-    def whiten(out, ref, counts):
-        total = jnp.zeros((n, 1), jnp.float32)
-        for c in range(CHUNKS):
-            part = ref[:n, c * width : (c + 1) * width].astype(jnp.float32)
-            total += jnp.sum(part * part, axis=1, keepdims=True)
+        part = jnp.where(usable(own_counts, c), strain[:, edges[c] : edges[c + 1]].astype(jnp.float32), 0.0)
+        xall[pl.ds(z * n, n), edges[c] : edges[c + 1]] = part.astype(jnp.bfloat16)
+
+    def energy(ref, c):
+        part = ref[:n, edges[c] : edges[c + 1]].astype(jnp.float32)
+        return jnp.sum(part * part, axis=1, keepdims=True)
+
+    def whiten(out, ref, counts, total):
         gain = 1.0 / jnp.sqrt(total / jnp.maximum(counts, 1.0) + epsilon)
         for c in range(CHUNKS):
-            part = ref[:n, c * width : (c + 1) * width].astype(jnp.float32)
-            out[:, c * width : (c + 1) * width] = (part * gain).astype(jnp.bfloat16)
+            part = ref[:n, edges[c] : edges[c + 1]].astype(jnp.float32)
+            out[:, edges[c] : edges[c + 1]] = (part * gain).astype(jnp.bfloat16)
 
     @pl.when(is_end)
     def _():
@@ -167,12 +198,19 @@
         for c in range(2, CHUNKS):
             mask_own(c)
             go(x_copy(z, EX, c, near))
-        for c in range(CHUNKS):
-            part_copy(fe, fe, FE, c, {"grp": near}).wait_recv()
-            part_copy(s_all, s_all, SE, c, {"grp": near}).wait_recv()
+        w_total = s_total = jnp.zeros((n, 1), jnp.float32)
+        for step in range(CHUNKS + 2):
+            if step < CHUNKS:
+                part_copy(fe, fe, FE, step, {"grp": near}).wait_recv()
+                w_total += energy(fe, step)
+            if step == CHUNKS - 1:
+                whiten(w_out, fe, own_counts, w_total)
+            if step >= 2:
+                part_copy(s_all, s_all, SE, step - 2, {"grp": near}).wait_recv()
+                s_total += energy(s_all, step - 2)
+        whiten(s_out, s_all, counts_column(s_all[n:, :n], n), s_total)
         for c in sends:
             c.wait_send()
-        whiten(w_out, fe, own_counts)
 
     @pl.when(jnp.logical_not(is_end))
     def _():
@@ -209,14 +247,14 @@
         end_counts = counts_column(mext_end[n:], n)
         m_copy(msel_far, msel_far, 2, far).wait_recv()
         left[2 * n : 3 * n] = msel_sum[:n] + msel_far[:n]
-        left[3 * n :] = pick[...]
+        left[3 * n :] = pick
         meta = msel_sum[n:] + msel_far[n:]
         src_counts = counts_column(meta, n)
         sa[n:] = jnp.zeros((META, samples), jnp.bfloat16)
         sa[n:, :n] = meta[:, :n]
 
         def process(c):
-            a, b = c * width, (c + 1) * width
+            a, b = edges[c], edges[c + 1]
             x_copy(far, XI, c, far).wait_recv()
             x_copy(far_end, XE, c, far).wait_recv()
             coupled = jnp.dot(left[...], xall[:, a:b], preferred_element_type=jnp.float32)
@@ -227,20 +265,23 @@
             sa[:n, a:b] = part.astype(jnp.bfloat16)
             go(part_copy(sa, ra, SA, c, {"seg": flips[0]}))
             go(part_copy(fe, fe, FE, c, {"grp": end}))
-            fown[:, a:b] = jnp.where(usable(own_counts, c), own_x - coupled[:n], 0.0)
+            own = jnp.where(usable(own_counts, c), own_x - coupled[:n], 0.0)
+            fown[:, a:b] = own
+            return jnp.sum(own * own, axis=1, keepdims=True)
 
         def stage(mine, arrived, total, kind, c, flip):
-            a, b = c * width, (c + 1) * width
+            a, b = edges[c], edges[c + 1]
             part_copy(mine, arrived, kind, c, {"seg": flip}).wait_recv()
             total[:, a:b] = mine[:, a:b] + arrived[:, a:b]
 
+        w_total = s_total = jnp.zeros((n, 1), jnp.float32)
         for step in range(CHUNKS + 3):
             if step + 2 < CHUNKS:
                 forward(step + 2)
             if step + 3 < CHUNKS:
                 send_own(step + 3)
             if step < CHUNKS:
-                process(step)
+                w_total += process(step)
             if 0 <= step - 1 < CHUNKS:
                 stage(sa, ra, sb, SA, step - 1, flips[0])
                 go(part_copy(sb, rb, SB, step - 1, {"seg": flips[1]}))
@@ -250,43 +291,26 @@
             if 0 <= step - 3 < CHUNKS:
                 stage(sc, rc, s_all, SC, step - 3, flips[2])
                 go(part_copy(s_all, s_all, SE, step - 3, {"grp": end}))
-        whiten(w_out, fown, own_counts)
+                s_total += energy(s_all, step - 3)
+            if step == CHUNKS:
+                whiten(w_out, fown, own_counts, w_total)
+        whiten(s_out, s_all, counts_column(s_all[n:, :n], n), s_total)
         for c in sends:
             c.wait_send()
-
-    whiten(s_out, s_all, counts_column(s_all[n:, :n], n))
 
 
 def gather(strain, counts, working, mixing, owners, offsets):
     n, samples = strain.shape
     wide = mixing.shape[1]
-    me = lax.axis_index(("seg", "grp"))
-    groups = wide // n
-    group = lax.axis_index("seg")
-    eff = jnp.where(working > 0, counts, 0)
-    meta = jnp.stack([eff // 8, eff % 8]).astype(jnp.bfloat16)
-    mext = jnp.concatenate([mixing, jnp.pad(meta, ((0, META - 2), (0, wide - n)))], axis=0)
-    rows, metas, picks = [], [], []
-    for r in range(ROUNDS):
-        here = me == owners[r]
-        rows.append(jnp.where(here, lax.dynamic_slice_in_dim(mixing, offsets[r], SRC, 0), 0))
-        metas.append(jnp.where(here, lax.dynamic_slice_in_dim(meta, offsets[r], SRC, 1), 0))
-        first = jnp.where(owners[r] // groups == group, (owners[r] % groups) * n + offsets[r], -wide)
-        column = lax.broadcasted_iota(jnp.int32, (SRC, wide), 1)
-        row = lax.broadcasted_iota(jnp.int32, (SRC, wide), 0)
-        picks.append(column == row + first)
-    sel_meta = jnp.concatenate(metas, axis=1)
-    msel = jnp.concatenate(rows + [jnp.pad(sel_meta, ((0, META - 2), (0, wide - n)))], axis=0).astype(jnp.bfloat16)
-    pick = jnp.concatenate(picks, axis=0).astype(jnp.bfloat16)
     vmem = pl.BlockSpec(memory_space=pltpu.VMEM)
     part = pltpu.VMEM((n + META, samples), jnp.bfloat16)
     mat = pltpu.VMEM((n + META, wide), jnp.bfloat16)
     return pl.pallas_call(
         gather_kernel,
         out_shape=[jax.ShapeDtypeStruct((n, samples), jnp.bfloat16)] * 2,
-        in_specs=[vmem] * 4,
+        in_specs=[pl.BlockSpec(memory_space=pltpu.SMEM)] * 2 + [vmem] * 4,
         out_specs=[vmem] * 2,
-        scratch_shapes=[
+        scratch_shapes=[mat] * 2 + [
             pltpu.VMEM((wide, samples), jnp.bfloat16),
             pltpu.VMEM((n, samples), jnp.float32),
             pltpu.VMEM((n, samples), jnp.bfloat16),
@@ -300,7 +324,7 @@
         compiler_params=pltpu.CompilerParams(
             collective_id=0, has_side_effects=True, vmem_limit_bytes=32 * 1024 * 1024),
         name="gather",
-    )(strain, mext, msel, pick)
+    )(owners, offsets, strain, counts.reshape(1, n), working.reshape(1, n), mixing)
 
 
 def gather_any(strain, counts, working, mixing, owners, offsets):

time: 87.8 us -> 73.2 us (0.83)
  between operations: 12.1 us -> 0.02 us
  other arithmetic: 2.93 us -> 0 us
    unnamed x2 -> x12, local copies, waits for them, and re-layouts: 1.01 us -> 4.54 us
    slice x2 -> x0, local copies, waits for them, and re-layouts: 2.76 us -> none  [the longest x1 1.38 us: gather(): here = me == owners[r]]
    pallas_call x1, Pallas kernels: 21.8 us -> 19.6 us  [correlate(): pl.pallas_call(correlate_kernel, out_shape=jax.ShapeDtypeStruct((ROUNDS,...]
    pallas_call x1, Pallas kernels: 46.8 us -> 48.8 us  [gather(): pl.pallas_call(gather_kernel, out_shape=[jax.ShapeDtypeStruct((n, samples...]
    select_n x2 -> x0, other arithmetic: 1.09 us -> none  [the longest x1 1.02 us: gather(): jnp.where(here, lax.dynamic_slice_in_dim(mixing, offsets[r], SRC, 0), 0)]
    concatenate x2 -> x0, other arithmetic: 1.01 us -> none  [the longest x1 0.93 us: gather(): jnp.concatenate([mixing, jnp.pad(meta, ((0, META - 2), (0, wide - n)))],...]
where the time goes in v3:
time: 73.2 us; the launch traced here: 73 us
  Pallas kernels  68.4 us (93%)
  local copies, waits for them, and re-layouts  4.54 us (6%)
    pallas_call x1, Pallas kernels, gather(): pl.pallas_call(gather_kernel, out_shape=[jax.ShapeDtypeStruct((n, samples...  48.8 us
    pallas_call x1, Pallas kernels, correlate(): pl.pallas_call(correlate_kernel, out_shape=jax.ShapeDtypeStruct((ROUNDS,...  19.6 us
    unnamed x12, local copies, waits for them, and re-layouts  4.54 us

profile of v3, /device:TPU:0, one launch (start us, length us, event | category | flops | bytes accessed | tf_op | source)
XLA Modules:
  0.0 73.0 jit_solution(6591084123026959543)
XLA Ops:
  0.0 0.0 copy-start
  0.0 1.0 %copy-done = bf16[128,1792]{1,0:T(8,128)(2,1)S(1)} copy-done((bf16[128,1792]{1,0:T(8,128)(2,1)S(1)}, bf16[128,1792]{1,0:T(8,128)(2,1)}, u32[]{:S(2)}) %copy-start) | copy-done | bytes 458776
  1.0 0.0 copy-start.1
  1.0 0.9 %copy-done.1 = bf16[128,512]{1,0:T(8,128)(2,1)S(1)} copy-done((bf16[128,512]{1,0:T(8,128)(2,1)S(1)}, bf16[128,512]{1,0:T(8,128)(2,1)}, u32[]{:S(2)}) %copy-start.1) | copy-done | bytes 131096
  1.9 0.0 copy-start.2
  1.9 0.7 copy-done.2
  2.6 0.0 copy-start.3
  2.6 0.7 copy-done.3
  3.2 0.0 copy-start.4
  3.2 0.7 copy-done.4
  3.9 0.0 copy-start.5
  3.9 0.7 copy-done.5
  4.5 48.8 %gather.1 = (bf16[128,1792]{1,0:T(8,128)(2,1)S(1)}, bf16[128,1792]{1,0:T(8,128)(2,1)S(1)}) custom-call(s32[2]{0:T(128)S(1)} %copy-done.2, s32[2]{0:T(128)S(1)} %copy-done.3, bf16[128,1792]{1,0:T(8,128)(2,1)S(1)} %copy-done, s32[1,128]{1,0:T(1,128)S(1)} %bitcast.2, s32[1,128]{1,0:T(1,128)S(1)} %bitcast.3, bf16[128,512]{1,0:T(8,128)(2,1)S(1)} %copy-done.1), custom_call_target="tpu_custom_call" | custom-call | tf_op jit(solution)/shard_map/gather/pallas_call | solution.py:308
  53.4 19.6 %correlate.1 = bf16[2,201,64,128]{3,2,1,0:T(8,128)(2,1)} custom-call(bf16[128,1792]{1,0:T(8,128)(2,1)S(1)} %get-tuple-element.7.w_ref, bf16[128,1792]{1,0:T(8,128)(2,1)S(1)} %get-tuple-element.8.s_ref), custom_call_target="tpu_custom_call" | custom-call | flops 11802771456 | bytes 8388608 | tf_op jit(solution)/shard_map/correlate/pallas_call | solution.py:68
Async XLA Ops:
  0.0 1.0 %copy-start = (bf16[128,1792]{1,0:T(8,128)(2,1)S(1)}, bf16[128,1792]{1,0:T(8,128)(2,1)}, u32[]{:S(2)}) copy-start(bf16[128,1792]{1,0:T(8,128)(2,1)} %strain.1) | copy-start | bytes 1376260
  1.0 0.9 %copy-start.1 = (bf16[128,512]{1,0:T(8,128)(2,1)S(1)}, bf16[128,512]{1,0:T(8,128)(2,1)}, u32[]{:S(2)}) copy-start(bf16[128,512]{1,0:T(8,128)(2,1)} %mixing.1) | copy-start | bytes 393220
  1.9 0.7 copy-start.2
  2.6 0.7 copy-start.3
  3.2 0.7 copy-start.4
  3.9 0.7 copy-start.5

commit v4 on v3

--- a/solution.py
+++ b/solution.py
@@ -17,15 +17,23 @@
 NT = (((1,), (1,)), ((), ()))
 
 
-def correlate_kernel(w_ref, s_ref, out_hbm, out_ref, wpad, spad, left, right, sem):
+def correlate_kernel(w_ref, s_ref, out_hbm, out_ref, wpad, spad, left, right, sem, in_sem):
     channels, samples = w_ref.shape
     rows = s_ref.shape[0]
     scale = 1.0 / float(samples) ** 0.5
-    for pad, ref in ((wpad, w_ref), (spad, s_ref)):
-        edge = jnp.zeros((ref.shape[0], PAD), ref.dtype)
+    middle = pl.ds(PAD, samples)
+    fetches = [
+        pltpu.make_async_copy(ref, pad.at[:, middle], in_sem.at[k])
+        for k, (pad, ref) in enumerate(((wpad, w_ref), (spad, s_ref)))
+    ]
+    for fetch in fetches:
+        fetch.start()
+    for pad in (wpad, spad):
+        edge = jnp.zeros((pad.shape[0], PAD), pad.dtype)
         pad[:, :PAD] = edge
         pad[:, PAD + samples :] = edge
-        pad[:, PAD : PAD + samples] = ref[...]
+    for fetch in fetches:
+        fetch.wait()
     for sign_index, sign in enumerate((1, -1)):
         for group in range(GROUPS):
             start = PAD + sign * STEP * group
@@ -34,31 +42,38 @@
             start = PAD - sign * (delta + 1)
             right[sign_index * STEP + delta] = wpad[:, start : start + samples]
 
-    centre = lax.dot_general(s_ref[...], w_ref[...], NT, preferred_element_type=jnp.float32)
+    centre = lax.dot_general(spad[:, middle], wpad[:, middle], NT, preferred_element_type=jnp.float32)
     centre = (centre * scale).astype(jnp.bfloat16)
     for r in range(ROUNDS):
         out_ref[r, LAG] = centre[r * SRC : (r + 1) * SRC]
         pltpu.make_async_copy(out_ref.at[r, LAG], out_hbm.at[r, LAG], sem).start()
 
-    def tile(n, carry):
-        sign_index = n // (STEP // 2)
-        sign = 1 - 2 * sign_index
-        first = (n % (STEP // 2)) * 2
-        pair = right[pl.ds(n * 2, 2)].reshape(2 * channels, samples)
-        products = lax.dot_general(left[sign_index], pair, NT, preferred_element_type=jnp.float32)
-        products = (products * scale).astype(jnp.bfloat16)
-        for group in range(GROUPS):
-            for r in range(ROUNDS):
-                row = group * rows + r * SRC
-                for d in range(2):
-                    lag = LAG + sign * (STEP * group + first + d + 1)
-                    out_ref[r, lag] = products[row : row + SRC, d * channels : (d + 1) * channels]
-                low = LAG + sign * (STEP * group + first) + 1 - 3 * sign_index
-                slab = (r, pl.ds(low, 2))
-                pltpu.make_async_copy(out_ref.at[slab], out_hbm.at[slab], sem).start()
+    half = STEP // 2
+
+    def tiles(n, carry):
+        results = []
+        for sign_index in range(2):
+            pair = right[pl.ds(sign_index * STEP + n * 2, 2)].reshape(2 * channels, samples)
+            products = lax.dot_general(left[sign_index], pair, NT, preferred_element_type=jnp.float32)
+            results.append((products * scale).astype(jnp.bfloat16))
+        for sign_index, products in enumerate(results):
+            for group in range(GROUPS):
+                for r in range(ROUNDS):
+                    row = group * rows + r * SRC
+                    for d in range(2):
+                        offset = STEP * group + 2 * n + d + 1
+                        lag = LAG + offset if sign_index == 0 else LAG - offset
+                        out_ref[r, lag] = products[row : row + SRC, d * channels : (d + 1) * channels]
+        for sign_index in range(2):
+            for group in range(GROUPS):
+                for r in range(ROUNDS):
+                    offset = STEP * group + 2 * n
+                    low = LAG + offset + 1 if sign_index == 0 else LAG - offset - 2
+                    slab = (r, pl.ds(low, 2))
+                    pltpu.make_async_copy(out_ref.at[slab], out_hbm.at[slab], sem).start()
         return carry
 
-    lax.fori_loop(0, STEP, tile, 0)
+    lax.fori_loop(0, half, tiles, 0)
     pltpu.make_async_copy(out_ref, out_hbm, sem).wait()
 
 
@@ -68,7 +83,7 @@
     return pl.pallas_call(
         correlate_kernel,
         out_shape=jax.ShapeDtypeStruct((ROUNDS, LAGS, SRC, channels), jnp.bfloat16),
-        in_specs=[pl.BlockSpec(memory_space=pltpu.VMEM)] * 2,
+        in_specs=[pl.BlockSpec(memory_space=pl.ANY)] * 2,
         out_specs=pl.BlockSpec(memory_space=pl.ANY),
         scratch_shapes=[
             pltpu.VMEM((ROUNDS, LAGS, SRC, channels), jnp.bfloat16),
@@ -77,8 +92,9 @@
             pltpu.VMEM((2, GROUPS * rows, samples), jnp.bfloat16),
             pltpu.VMEM((2 * STEP, channels, samples), jnp.bfloat16),
             pltpu.SemaphoreType.DMA,
+            pltpu.SemaphoreType.DMA((2,)),
         ],
-        compiler_params=pltpu.CompilerParams(vmem_limit_bytes=52 * 1024 * 1024),
+        compiler_params=pltpu.CompilerParams(vmem_limit_bytes=56 * 1024 * 1024),
         cost_estimate=pl.CostEstimate(
             flops=2 * LAGS * rows * channels * samples, bytes_accessed=8 << 20, transcendentals=0
         ),
@@ -100,7 +116,8 @@
     return jnp.sum(jnp.where(row == lane, lanes, 0.0), axis=1, keepdims=True)
 
 
-def gather_kernel(owners, offsets, strain, counts, working, mixing, w_out, s_out, mext, msel, xall, fown, fe, sa, ra, sb, rb, sc, rc,
+def gather_kernel(owners_hbm, offsets_hbm, strain_hbm, counts_hbm, working_hbm, mixing_hbm, w_out, s_out,
+                  owners, offsets, strain, counts, working, mixing, in_sem, mext, msel, xall, fown, fe, sa, ra, sb, rb, sc, rc,
                   s_all, mext_end, msel_end, msel_sum, msel_far, left, send, recv, msend, mrecv):
     n, samples = strain.shape
     wide = mixing.shape[1]
@@ -137,7 +154,28 @@
             src_ref=src, dst_ref=dst, send_sem=msend.at[index], recv_sem=mrecv.at[index],
             device_id={"grp": target}, device_id_type=MESH)
 
+    fetches = [
+        pltpu.make_async_copy(a, b, in_sem.at[k])
+        for k, (a, b) in enumerate(((owners_hbm, owners), (offsets_hbm, offsets), (counts_hbm, counts),
+                                    (working_hbm, working), (mixing_hbm, mixing), (strain_hbm, strain)))
+    ]
+    for fetch in fetches:
+        fetch.start()
     barrier = pltpu.get_barrier_semaphore()
+
+    @pl.when(is_end)
+    def _():
+        pl.semaphore_signal(barrier, inc=1, device_id={"grp": near}, device_id_type=MESH)
+
+    @pl.when(jnp.logical_not(is_end))
+    def _():
+        for target in (end, far):
+            pl.semaphore_signal(barrier, inc=1, device_id={"grp": target}, device_id_type=MESH)
+        for target in flips:
+            pl.semaphore_signal(barrier, inc=1, device_id={"seg": target}, device_id_type=MESH)
+
+    for fetch in fetches:
+        fetch.wait()
     live = jnp.where(working[...] > 0, counts[...], 0)
     high = live // 8
     row = lax.broadcasted_iota(jnp.int32, (META, n), 0)
@@ -181,7 +219,6 @@
 
     @pl.when(is_end)
     def _():
-        pl.semaphore_signal(barrier, inc=1, device_id={"grp": near}, device_id_type=MESH)
         pl.semaphore_wait(barrier, 1)
         sends = []
 
@@ -214,10 +251,6 @@
 
     @pl.when(jnp.logical_not(is_end))
     def _():
-        for target in (end, far):
-            pl.semaphore_signal(barrier, inc=1, device_id={"grp": target}, device_id_type=MESH)
-        for target in flips:
-            pl.semaphore_signal(barrier, inc=1, device_id={"seg": target}, device_id_type=MESH)
         pl.semaphore_wait(barrier, 5)
         sends = []
 
@@ -308,9 +341,15 @@
     return pl.pallas_call(
         gather_kernel,
         out_shape=[jax.ShapeDtypeStruct((n, samples), jnp.bfloat16)] * 2,
-        in_specs=[pl.BlockSpec(memory_space=pltpu.SMEM)] * 2 + [vmem] * 4,
+        in_specs=[pl.BlockSpec(memory_space=pl.ANY)] * 6,
         out_specs=[vmem] * 2,
-        scratch_shapes=[mat] * 2 + [
+        scratch_shapes=[pltpu.SMEM((ROUNDS,), jnp.int32)] * 2 + [
+            pltpu.VMEM((n, samples), jnp.bfloat16),
+            pltpu.VMEM((1, n), jnp.int32),
+            pltpu.VMEM((1, n), jnp.int32),
+            pltpu.VMEM((n, wide), jnp.bfloat16),
+            pltpu.SemaphoreType.DMA((6,)),
+        ] + [mat] * 2 + [
             pltpu.VMEM((wide, samples), jnp.bfloat16),
             pltpu.VMEM((n, samples), jnp.float32),
             pltpu.VMEM((n, samples), jnp.bfloat16),
@@ -322,7 +361,7 @@
             pltpu.SemaphoreType.DMA((3,)),
         ],
         compiler_params=pltpu.CompilerParams(
-            collective_id=0, has_side_effects=True, vmem_limit_bytes=32 * 1024 * 1024),
+            collective_id=0, has_side_effects=True, vmem_limit_bytes=56 * 1024 * 1024),
         name="gather",
     )(owners, offsets, strain, counts.reshape(1, n), working.reshape(1, n), mixing)
 

time: 73.2 us -> 71.1 us (0.971)
  local copies, waits for them, and re-layouts: 4.54 us -> 0 us
  Pallas kernels: 68.4 us -> 70.9 us
    unnamed x12 -> x0, local copies, waits for them, and re-layouts: 4.54 us -> none
    pallas_call x1, Pallas kernels: 48.8 us -> 50.2 us  [gather(): pl.pallas_call(gather_kernel, out_shape=[jax.ShapeDtypeStruct((n, samples...]
    pallas_call x1, Pallas kernels: 19.6 us -> 20.7 us  [correlate(): pl.pallas_call(correlate_kernel, out_shape=jax.ShapeDtypeStruct((ROUNDS,...]
where the time goes in v4:
time: 71.1 us; the launch traced here: 70.9 us
  Pallas kernels  70.9 us (100%)
    pallas_call x1, Pallas kernels, gather(): pl.pallas_call(gather_kernel, out_shape=[jax.ShapeDtypeStruct((n, samples...  50.2 us
    pallas_call x1, Pallas kernels, correlate(): pl.pallas_call(correlate_kernel, out_shape=jax.ShapeDtypeStruct((ROUNDS,...  20.7 us

profile of v4, /device:TPU:0, one launch (start us, length us, event | category | flops | bytes accessed | tf_op | source)
XLA Modules:
  0.0 70.9 jit_solution(7399953912858068760)
XLA Ops:
  0.0 50.2 %gather.1 = (bf16[128,1792]{1,0:T(8,128)(2,1)}, bf16[128,1792]{1,0:T(8,128)(2,1)}) custom-call(s32[2]{0:T(128)} %owners_hbm.1, s32[2]{0:T(128)} %offsets_hbm.1, bf16[128,1792]{1,0:T(8,128)(2,1)} %strain_hbm.1, s32[1,128]{1,0:T(1,128)} %bitcast.2, s32[1,128]{1,0:T(1,128)} %bitcast.3, bf16[128,512]{1,0:T(8,128)(2,1)} %mixing_hbm.1), custom_call_target="tpu_custom_call" | custom-call | tf_op jit(solution)/shard_map/gather/pallas_call | solution.py:341
  50.2 20.7 %correlate.1 = bf16[2,201,64,128]{3,2,1,0:T(8,128)(2,1)} custom-call(bf16[128,1792]{1,0:T(8,128)(2,1)} %get-tuple-element.7.w_ref, bf16[128,1792]{1,0:T(8,128)(2,1)} %get-tuple-element.8.s_ref), custom_call_target="tpu_custom_call" | custom-call | flops 11802771456 | bytes 8388608 | tf_op jit(solution)/shard_map/correlate/pallas_call | solution.py:83

commit v5 on v4

--- a/solution.py
+++ b/solution.py
@@ -9,7 +9,7 @@
 LAG = 100
 ROUNDS = 2
 LAGS = 201
-STEP = 10
+STEP = 4
 GROUPS = LAG // STEP
 PAD = 128
 
@@ -51,12 +51,10 @@
     half = STEP // 2
 
     def tiles(n, carry):
-        results = []
         for sign_index in range(2):
             pair = right[pl.ds(sign_index * STEP + n * 2, 2)].reshape(2 * channels, samples)
             products = lax.dot_general(left[sign_index], pair, NT, preferred_element_type=jnp.float32)
-            results.append((products * scale).astype(jnp.bfloat16))
-        for sign_index, products in enumerate(results):
+            products = (products * scale).astype(jnp.bfloat16)
             for group in range(GROUPS):
                 for r in range(ROUNDS):
                     row = group * rows + r * SRC
@@ -64,9 +62,6 @@
                         offset = STEP * group + 2 * n + d + 1
                         lag = LAG + offset if sign_index == 0 else LAG - offset
                         out_ref[r, lag] = products[row : row + SRC, d * channels : (d + 1) * channels]
-        for sign_index in range(2):
-            for group in range(GROUPS):
-                for r in range(ROUNDS):
                     offset = STEP * group + 2 * n
                     low = LAG + offset + 1 if sign_index == 0 else LAG - offset - 2
                     slab = (r, pl.ds(low, 2))
@@ -274,6 +269,8 @@
         go(m_copy(msel_sum, msel_far, 2, far))
         forward(1)
         send_own(2)
+        forward(2)
+        send_own(3)
         m_copy(mext_end, mext_end, 1, end).wait_recv()
         left[:n] = mext[:n]
         left[n : 2 * n] = mext_end[:n]
@@ -309,10 +306,10 @@
 
         w_total = s_total = jnp.zeros((n, 1), jnp.float32)
         for step in range(CHUNKS + 3):
-            if step + 2 < CHUNKS:
-                forward(step + 2)
             if step + 3 < CHUNKS:
-                send_own(step + 3)
+                forward(step + 3)
+            if step + 4 < CHUNKS:
+                send_own(step + 4)
             if step < CHUNKS:
                 w_total += process(step)
             if 0 <= step - 1 < CHUNKS:

time: 71.1 us -> 73.5 us (1.034)
  Pallas kernels: 70.9 us -> 73.1 us
    pallas_call x1, Pallas kernels: 20.7 us -> 22.7 us  [correlate(): pl.pallas_call(correlate_kernel, out_shape=jax.ShapeDtypeStruct((ROUNDS,...]
where the time goes in v5:
time: 73.5 us; the launch traced here: 73.3 us
  Pallas kernels  73.1 us (99%)
    pallas_call x1, Pallas kernels, gather(): pl.pallas_call(gather_kernel, out_shape=[jax.ShapeDtypeStruct((n, samples...  50.4 us
    pallas_call x1, Pallas kernels, correlate(): pl.pallas_call(correlate_kernel, out_shape=jax.ShapeDtypeStruct((ROUNDS,...  22.7 us

profile of v5, /device:TPU:0, one launch (start us, length us, event | category | flops | bytes accessed | tf_op | source)
XLA Modules:
  0.0 73.3 jit_solution(9162337987770133884)
XLA Ops:
  0.0 50.4 %gather.1 = (bf16[128,1792]{1,0:T(8,128)(2,1)}, bf16[128,1792]{1,0:T(8,128)(2,1)}) custom-call(s32[2]{0:T(128)} %owners_hbm.1, s32[2]{0:T(128)} %offsets_hbm.1, bf16[128,1792]{1,0:T(8,128)(2,1)} %strain_hbm.1, s32[1,128]{1,0:T(1,128)} %bitcast.2, s32[1,128]{1,0:T(1,128)} %bitcast.3, bf16[128,512]{1,0:T(8,128)(2,1)} %mixing_hbm.1), custom_call_target="tpu_custom_call" | custom-call | tf_op jit(solution)/shard_map/gather/pallas_call | solution.py:338
  50.5 22.7 %correlate.1 = bf16[2,201,64,128]{3,2,1,0:T(8,128)(2,1)} custom-call(bf16[128,1792]{1,0:T(8,128)(2,1)} %get-tuple-element.7.w_ref, bf16[128,1792]{1,0:T(8,128)(2,1)} %get-tuple-element.8.s_ref), custom_call_target="tpu_custom_call" | custom-call | flops 11802771456 | bytes 8388608 | tf_op jit(solution)/shard_map/correlate/pallas_call | solution.py:78

commit v6 on v4

--- a/solution.py
+++ b/solution.py
@@ -34,13 +34,20 @@
         pad[:, PAD + samples :] = edge
     for fetch in fetches:
         fetch.wait()
-    for sign_index, sign in enumerate((1, -1)):
-        for group in range(GROUPS):
-            start = PAD + sign * STEP * group
-            left[sign_index, group * rows : (group + 1) * rows, :] = spad[:, start : start + samples]
-        for delta in range(STEP):
-            start = PAD - sign * (delta + 1)
-            right[sign_index * STEP + delta] = wpad[:, start : start + samples]
+    half = STEP // 2
+
+    def shift_sources(sign_index, group):
+        start = PAD + (1 - 2 * sign_index) * STEP * group
+        left[sign_index, group * rows : (group + 1) * rows, :] = spad[:, start : start + samples]
+
+    def shift_pair(tile):
+        for delta in (2 * (tile % half), 2 * (tile % half) + 1):
+            start = PAD - (1 - 2 * (tile // half)) * (delta + 1)
+            right[tile // half * STEP + delta] = wpad[:, start : start + samples]
+
+    shift_pair(0)
+    for group in range(GROUPS):
+        shift_sources(0, group)
 
     centre = lax.dot_general(spad[:, middle], wpad[:, middle], NT, preferred_element_type=jnp.float32)
     centre = (centre * scale).astype(jnp.bfloat16)
@@ -48,32 +55,27 @@
         out_ref[r, LAG] = centre[r * SRC : (r + 1) * SRC]
         pltpu.make_async_copy(out_ref.at[r, LAG], out_hbm.at[r, LAG], sem).start()
 
-    half = STEP // 2
-
-    def tiles(n, carry):
-        results = []
-        for sign_index in range(2):
-            pair = right[pl.ds(sign_index * STEP + n * 2, 2)].reshape(2 * channels, samples)
-            products = lax.dot_general(left[sign_index], pair, NT, preferred_element_type=jnp.float32)
-            results.append((products * scale).astype(jnp.bfloat16))
-        for sign_index, products in enumerate(results):
-            for group in range(GROUPS):
-                for r in range(ROUNDS):
-                    row = group * rows + r * SRC
-                    for d in range(2):
-                        offset = STEP * group + 2 * n + d + 1
-                        lag = LAG + offset if sign_index == 0 else LAG - offset
-                        out_ref[r, lag] = products[row : row + SRC, d * channels : (d + 1) * channels]
-        for sign_index in range(2):
-            for group in range(GROUPS):
-                for r in range(ROUNDS):
-                    offset = STEP * group + 2 * n
-                    low = LAG + offset + 1 if sign_index == 0 else LAG - offset - 2
-                    slab = (r, pl.ds(low, 2))
-                    pltpu.make_async_copy(out_ref.at[slab], out_hbm.at[slab], sem).start()
-        return carry
-
-    lax.fori_loop(0, half, tiles, 0)
+    for tile in range(2 * half):
+        sign_index, n = tile // half, tile % half
+        if tile + 1 < 2 * half:
+            shift_pair(tile + 1)
+        if sign_index == 0:
+            shift_sources(1, 2 * n)
+            shift_sources(1, 2 * n + 1)
+        pair = right[2 * tile : 2 * tile + 2].reshape(2 * channels, samples)
+        products = lax.dot_general(left[sign_index], pair, NT, preferred_element_type=jnp.float32)
+        products = (products * scale).astype(jnp.bfloat16)
+        slabs = []
+        for group in range(GROUPS):
+            for r in range(ROUNDS):
+                row = group * rows + r * SRC
+                offset = STEP * group + 2 * n
+                for d in range(2):
+                    lag = LAG + (1 - 2 * sign_index) * (offset + d + 1)
+                    out_ref[r, lag] = products[row : row + SRC, d * channels : (d + 1) * channels]
+                slabs.append((r, pl.ds(LAG + offset + 1 if sign_index == 0 else LAG - offset - 2, 2)))
+        for slab in slabs:
+            pltpu.make_async_copy(out_ref.at[slab], out_hbm.at[slab], sem).start()
     pltpu.make_async_copy(out_ref, out_hbm, sem).wait()
 
 

time: 71.1 us -> 65.6 us (0.923)
  Pallas kernels: 70.9 us -> 65.2 us
    pallas_call x1, Pallas kernels: 20.7 us -> 14.9 us  [correlate(): pl.pallas_call(correlate_kernel, out_shape=jax.ShapeDtypeStruct((ROUNDS,...]
where the time goes in v6:
time: 65.6 us; the launch traced here: 65.4 us
  Pallas kernels  65.2 us (99%)
    pallas_call x1, Pallas kernels, gather(): pl.pallas_call(gather_kernel, out_shape=[jax.ShapeDtypeStruct((n, samples...  50.4 us
    pallas_call x1, Pallas kernels, correlate(): pl.pallas_call(correlate_kernel, out_shape=jax.ShapeDtypeStruct((ROUNDS,...  14.9 us

profile of v6, /device:TPU:0, one launch (start us, length us, event | category | flops | bytes accessed | tf_op | source)
XLA Modules:
  0.0 65.4 jit_solution(6817958529191024010)
XLA Ops:
  0.0 50.4 %gather.1 = (bf16[128,1792]{1,0:T(8,128)(2,1)}, bf16[128,1792]{1,0:T(8,128)(2,1)}) custom-call(s32[2]{0:T(128)} %owners_hbm.1, s32[2]{0:T(128)} %offsets_hbm.1, bf16[128,1792]{1,0:T(8,128)(2,1)} %strain_hbm.1, s32[1,128]{1,0:T(1,128)} %bitcast.2, s32[1,128]{1,0:T(1,128)} %bitcast.3, bf16[128,512]{1,0:T(8,128)(2,1)} %mixing_hbm.1), custom_call_target="tpu_custom_call" | custom-call | tf_op jit(solution)/shard_map/gather/pallas_call | solution.py:343
  50.4 14.9 %correlate.1 = bf16[2,201,64,128]{3,2,1,0:T(8,128)(2,1)} custom-call(bf16[128,1792]{1,0:T(8,128)(2,1)} %get-tuple-element.7.w_ref, bf16[128,1792]{1,0:T(8,128)(2,1)} %get-tuple-element.8.s_ref), custom_call_target="tpu_custom_call" | custom-call | flops 11802771456 | bytes 8388608 | tf_op jit(solution)/shard_map/correlate/pallas_call | solution.py:85

commit v7 on v6

--- a/solution.py
+++ b/solution.py
@@ -104,7 +104,7 @@
     )(whitened, sources)
 
 
-EDGES = (0, 2, 4, 6, 8, 10, 12, 13, 14)
+EDGES = (0, 2, 4, 6, 8, 10, 11, 12, 13, 14)
 CHUNKS = len(EDGES) - 1
 META = 16
 XI, XE, EX, FE, SA, SB, SC, SE = range(8)

time: 65.6 us -> 67.1 us (1.023)
  Pallas kernels: 65.2 us -> 66.8 us
    pallas_call x1, Pallas kernels: 50.4 us -> 52 us  [gather(): pl.pallas_call(gather_kernel, out_shape=[jax.ShapeDtypeStruct((n, samples...]
where the time goes in v7:
time: 67.1 us; the launch traced here: 67 us
  Pallas kernels  66.8 us (100%)
    pallas_call x1, Pallas kernels, gather(): pl.pallas_call(gather_kernel, out_shape=[jax.ShapeDtypeStruct((n, samples...  52 us
    pallas_call x1, Pallas kernels, correlate(): pl.pallas_call(correlate_kernel, out_shape=jax.ShapeDtypeStruct((ROUNDS,...  14.9 us

profile of v7, /device:TPU:0, one launch (start us, length us, event | category | flops | bytes accessed | tf_op | source)
XLA Modules:
  0.0 67.0 jit_solution(6012639152571397696)
XLA Ops:
  0.0 52.0 %gather.1 = (bf16[128,1792]{1,0:T(8,128)(2,1)}, bf16[128,1792]{1,0:T(8,128)(2,1)}) custom-call(s32[2]{0:T(128)} %owners_hbm.1, s32[2]{0:T(128)} %offsets_hbm.1, bf16[128,1792]{1,0:T(8,128)(2,1)} %strain_hbm.1, s32[1,128]{1,0:T(1,128)} %bitcast.2, s32[1,128]{1,0:T(1,128)} %bitcast.3, bf16[128,512]{1,0:T(8,128)(2,1)} %mixing_hbm.1), custom_call_target="tpu_custom_call" | custom-call | tf_op jit(solution)/shard_map/gather/pallas_call | solution.py:343
  52.0 14.9 %correlate.1 = bf16[2,201,64,128]{3,2,1,0:T(8,128)(2,1)} custom-call(bf16[128,1792]{1,0:T(8,128)(2,1)} %get-tuple-element.7.w_ref, bf16[128,1792]{1,0:T(8,128)(2,1)} %get-tuple-element.8.s_ref), custom_call_target="tpu_custom_call" | custom-call | flops 11802771456 | bytes 8388608 | tf_op jit(solution)/shard_map/correlate/pallas_call | solution.py:85
